TPU v7x, 768 devices: a whole 4x8x12 slice. The times are simulated.
768 devices in a mesh: mp: 12 (over z_lo, x), dp: 64 (over z_hi, y, core).
Axes of the slice: x: 4, y: 8, z: 12 (z_hi: 4, z_lo: 3; z = z_hi * 3 + z_lo), core: 2. Of those that a mesh axis runs over, the one named last changes fastest.
Arguments:
- hidden_pre: bfloat16 [512, 30720], P('dp', 'mp'), may hold values from -36 to 36
- grad_out: bfloat16 [512, 14848], P('dp'), may hold values from -90 to 90
- w_down: bfloat16 [30720, 14848], P('mp', 'dp'), may hold values from -0.046875 to 0.046875
Outputs:
- grad_pre: bfloat16 [512, 30720], P('dp', 'mp')
- grad_down: bfloat16 [30720, 14848], P('mp', 'dp')
All inputs are finite; a program needn't handle non-finite values.
Results may differ from a plain program's by a relative error of at most 0.004.
Values may be sent and summed in bfloat16 or wider, within the bound.
A program may use at most 32 MiB of HBM per device.

v0:
```python
import jax
import jax.numpy as jnp
from jax import lax
from jax.sharding import PartitionSpec as P

root_half = 0.7071067811865476
inv_root_tau = 0.3989422804014327


def gelu_value(value):
    return 0.5 * value * (1.0 + lax.erf(value * root_half))


def gelu_slope(value):
    return (
        0.5 * (1.0 + lax.erf(value * root_half))
        + value * jnp.exp(-0.5 * value * value) * inv_root_tau
    )


def row_products(tok_rows, w_down):
    return lax.dot_general(
        tok_rows, w_down, (((1,), (1,)), ((), ())), preferred_element_type=jnp.float32
    )


def weight_terms(hidden_rows, dy_rows):
    act = gelu_value(hidden_rows.astype(jnp.float32)).astype(jnp.bfloat16)
    return lax.dot_general(
        act, dy_rows, (((0,), (0,)), ((), ())), preferred_element_type=jnp.float32
    )


def local(hidden_pre, grad_out, w_down):
    dy_cols = lax.all_to_all(grad_out, "dp", split_axis=1, concat_axis=0, tiled=True)
    dy_hidden = lax.psum_scatter(
        row_products(dy_cols, w_down), "dp", scatter_dimension=0, tiled=True
    )
    grad_pre = (dy_hidden * gelu_slope(hidden_pre.astype(jnp.float32))).astype(jnp.bfloat16)
    hidden_all = lax.all_gather(hidden_pre, "dp", axis=0, tiled=True)
    raw = weight_terms(hidden_all, dy_cols)
    sumsq = lax.psum(jnp.sum(raw * raw), ("mp", "dp"))
    entries = float(w_down.shape[0] * lax.axis_size("mp")) * float(
        w_down.shape[1] * lax.axis_size("dp")
    )
    rms = jnp.sqrt(sumsq / entries + 1e-06)
    grad_down = (raw * jnp.minimum(1.0, 1.0 / rms)).astype(jnp.bfloat16)
    return (grad_pre, grad_down)


def solution(mesh):
    placed = (P("dp", "mp"), P("dp", None), P("mp", "dp"))
    return jax.shard_map(
        local, mesh=mesh, in_specs=placed, out_specs=(P("dp", "mp"), P("mp", "dp")), check_vma=False
    )
```

profile of v0, /device:TPU:1, one launch (start us, length us, event | category | flops | bytes accessed | tf_op | source)
XLA Modules:
  0.0 298.2 jit_solution(10345546301000107750)
XLA Ops:
  7.2 0.0 copy-start
  7.2 0.0 all-gather.2.cloned.1.call-start
  7.2 0.7 all-gather.2.cloned.1.call-update
  7.9 0.0 reduce-scatter.2.cloned.1.call-start
  8.0 1.7 all_to_all.14
  9.7 0.2 copy.5
  9.9 37.1 %all_to_all.19 = bf16[8,64,232]{2,0,1:T(8,128)(2,1)S(1)} all-to-all(bf16[8,64,232]{2,0,1:T(8,128)(2,1)S(1)} %copy.5), channel_id=1, replica_groups=mesh['mp'=12,'dp'=64] {'dp'}, dimensions={1} | all-to-all | bytes 475136 | tf_op jit(solution)/shard_map/all_to_all | solution.py:35
  47.0 0.0 copy-done
  47.0 3.2 %fusion.7 = f32[512,2560]{1,0:T(8,128)} fusion(bf16[2560,232]{0,1:T(8,128)(2,1)S(1)} %copy-done, bf16[8,64,232]{2,0,1:T(8,128)(2,1)S(1)} %all_to_all.19), kind=kOutput, calls=%fused_computation.10 | convolution fusion | flops 608174080 | bytes 6668288 | tf_op jit(solution)/shard_map/dot_general | solution.py:22
  50.1 0.0 reduce-scatter.2.cloned.1.call-update
  50.2 66.9 %all-gather.2.cloned.1.call-done = bf16[512,2560]{1,0:T(8,128)(2,1)} async-done(((bf16[8,2560]{1,0:T(8,128)(2,1)}), bf16[512,2560]{1,0:T(8,128)(2,1)}) %all-gather.2.cloned.1.call-update) | async-done | bytes 2621456 | tf_op jit(solution)/shard_map/all_gather | solution.py:40
  117.0 4.8 %multiply_reduce_fusion = (f32[]{:T(128)}, f32[2560,232]{0,1:T(8,128)}) fusion(bf16[8,64,232]{2,0,1:T(8,128)(2,1)S(1)} %all_to_all.19, bf16[512,2560]{1,0:T(8,128)(2,1)} %all-gather.2.cloned.1.call-done), kind=kOutput, calls=%fused_computation.8 | convolution fusion | flops 617226240 | bytes 5234692 | tf_op jit(solution)/shard_map/dot_general | solution.py:29
  121.9 0.0 copy-start.1
  121.9 107.0 %psum.7 = f32[]{:T(128)} all-reduce(f32[]{:T(128)} %get-tuple-element.2), channel_id=1, replica_groups=mesh['mp'=12,'dp'=64] {'mp','dp'}, use_global_device_ids=true, to_apply=%region_2.0 | all-reduce | flops 1 | bytes 8 | tf_op jit(solution)/shard_map/psum | solution.py:42
  229.6 2.9 multiply_convert_fusion
  232.4 57.4 %reduce-scatter.2.cloned.1.call-done = f32[8,2560]{1,0:T(8,128)} async-done(((f32[512,2560]{1,0:T(8,128)}), f32[8,2560]{1,0:T(8,128)}) %reduce-scatter.2.cloned.1.call-update) | async-done | bytes 81936 | tf_op jit(solution)/shard_map/reduce_scatter | solution.py:36
  289.8 0.0 copy-done.1
  289.8 1.5 fusion.16
Async XLA Ops:
  7.2 39.8 %copy-start = (bf16[2560,232]{0,1:T(8,128)(2,1)S(1)}, bf16[2560,232]{0,1:T(8,128)(2,1)}, u32[]{:S(2)}) copy-start(bf16[2560,232]{0,1:T(8,128)(2,1)} %param.5) | copy-start | bytes 3563524
  7.2 109.8 %all-gather.2.cloned.1.call-start = ((), (), s32[]{:S(2)}) async-start(), calls=%async_computation.3 | async-start | bytes 2662400 | tf_op jit(solution)/shard_map/all_gather | solution.py:40
  7.9 281.9 %reduce-scatter.2.cloned.1.call-start = ((), (), s32[]{:S(2)}) async-start(), calls=%async_computation.2 | async-start | bytes 5324800 | tf_op jit(solution)/shard_map/reduce_scatter | solution.py:36
  121.9 168.0 %copy-start.1 = (bf16[8,2560]{1,0:T(8,128)(2,1)S(1)}, bf16[8,2560]{1,0:T(8,128)(2,1)}, u32[]{:S(2)}) copy-start(bf16[8,2560]{1,0:T(8,128)(2,1)} %param.3) | copy-start | bytes 122884
Sparse Core Ops, SparseCore 0:
  11.9 105.0 all-gather.1
  122.3 167.4 reduce-scatter.1
where the time goes:
time: 302 us; the launch traced here: 298 us
  blocking collectives  144 us (48%)
  waiting for transfers between devices  125 us (41%)
  between operations  14.8 us (5%)
  matrix products  7.99 us (3%)
  other arithmetic  4.4 us (1%)
    psum x1, blocking collectives, local(): sumsq = lax.psum(jnp.sum(raw * raw), ('mp', 'dp'))  107 us
    all_gather x1, waiting for transfers between devices, local(): hidden_all = lax.all_gather(hidden_pre, 'dp', axis=0, tiled=True)  66.9 us
    reduce_scatter x1, waiting for transfers between devices, local(): lax.psum_scatter(row_products(dy_cols, w_down), 'dp', scatter_dimension=0...  57.4 us
    all_to_all x1, blocking collectives, local(): lax.all_to_all(grad_out, 'dp', split_axis=1, concat_axis=0, tiled=True)  37.1 us
  transfers between devices with their start and end apart: 2, of which 2 were waited for; matrix products, arithmetic and copies ran while one was open for 4% of the time, Pallas kernels for 0%

commit v1 on v0

v1 whole, which is shorter than its diff:
```python
import functools

import jax
import jax.numpy as jnp
from jax import lax
from jax.experimental import pallas as pl
from jax.experimental.pallas import tpu as pltpu
from jax.sharding import PartitionSpec as P

root_half = 0.7071067811865476
inv_root_tau = 0.3989422804014327

f32, bf16 = jnp.float32, jnp.bfloat16
MESH = pl.DeviceIdType.MESH

NX, NZL, NY, NZH = 4, 3, 8, 4
D, FF, TOKENS = 14848, 30720, 512
WIDE = 232
HALF = 1280
CHUNK = 256
NK = HALF // CHUNK
DZ = (0, 1, 3, 2)


def gelu_value(value):
    return 0.5 * value * (1.0 + lax.erf(value * root_half))


def gelu_slope(value):
    return (
        0.5 * (1.0 + lax.erf(value * root_half))
        + value * jnp.exp(-0.5 * value * value) * inv_root_tau
    )


def kernel(
    h_ref, g_ref, w_ref, gp_ref, gd_ref,
    slope, act_f, act_in, pf, pf_in, q, qin, gf, a_all, w_own, w_in, wp,
    dyp, sb, rb, zs, zr, fin, fin_in, raw, raw_in, gdv, ar_src, ar_in,
    local_sem, pair_s, pair_r, raw_s, raw_r, gy_s, gy_r, gz_s, gz_r, gx_s, gx_r,
    gd_s, gd_r, ay_s, ay_r, az_s, az_r, rs_s, rs_r, rz_s, rz_r, ar_s, ar_r,
):
    mp, dp = lax.axis_index("mp"), lax.axis_index("dp")
    x, zl = mp % NX, mp // NX
    c, y, zh = dp % 2, (dp // 2) % NY, dp // (2 * NY)
    oc = 1 - c

    def at(x_=None, zl_=None, c_=None, y_=None, zh_=None):
        x_ = x if x_ is None else x_
        zl_ = zl if zl_ is None else zl_
        c_ = c if c_ is None else c_
        y_ = y if y_ is None else y_
        zh_ = zh if zh_ is None else zh_
        return (zl_ * NX + x_, (zh_ * NY + y_) * 2 + c_)

    pair = at(c_=oc)
    later = []

    def copy(src, dst, ss, rs, to):
        return pltpu.make_async_remote_copy(
            src_ref=src, dst_ref=dst, send_sem=ss, recv_sem=rs, device_id=to, device_id_type=MESH
        )

    def send(src, dst, ss, rs, to):
        cp = copy(src, dst, ss, rs, to)
        cp.start()
        later.append(cp)

    def arrived(dst, ss, rs):
        copy(dst, dst, ss, rs, pair).wait_recv()

    barrier = pltpu.get_barrier_semaphore()
    peers = [pair]
    peers += [at(x_=(x + r) % NX) for r in range(1, NX)]
    peers += [at(y_=(y + r) % NY) for r in range(1, NY)]
    peers += [at(zh_=(zh + r) % NZH) for r in range(1, NZH)]
    peers += [at(zl_=(zl + r) % NZL) for r in range(1, NZL)]
    for peer in peers:
        pl.semaphore_signal(barrier, inc=1, device_id=peer, device_id_type=MESH)

    own_rows = pl.ds(pl.multiple_of(HALF * c, 16), HALF)
    other_rows = pl.ds(pl.multiple_of(HALF * oc, 16), HALF)
    w_copy = pltpu.make_async_copy(w_ref.at[own_rows], w_own, local_sem.at[0])
    w_copy.start()

    for half in range(2):
        hidden = h_ref[:, HALF * half:HALF * (half + 1)].astype(f32)
        act_f[half] = gelu_value(hidden).astype(bf16).astype(f32)
        slope[half] = gelu_slope(hidden)

    tile = x % 2
    first = WIDE * (x // 2) + 128 * tile
    lanes = lax.broadcasted_iota(jnp.int32, (8, 128), 1)
    keep = lanes < 128 - (256 - WIDE) * tile
    for d in range(NZH * NY):
        if d < NZH * NY - 1:
            off = 2 * WIDE * d + first
            start, width = (off // 128) * 128, 256
            window = g_ref[:, pl.ds(pl.multiple_of(start, 128), width)]
        else:
            off = 2 * WIDE * d + first
            start, width = D - 512, 512
            window = g_ref[:, start:start + width]
        rolled = pltpu.roll(window.astype(f32), width - (off - start), axis=1)
        pf[d] = jnp.where(keep, rolled[:, :128], 0.0)

    pl.semaphore_wait(barrier, len(peers))

    send(act_f.at[oc], act_in, pair_s.at[0], pair_r.at[0], pair)
    send(pf.at[pl.ds(16 * oc, 16)], pf_in, pair_s.at[1], pair_r.at[1], pair)
    send(w_ref.at[other_rows], w_in, pair_s.at[2], pair_r.at[2], pair)

    def rows_of(ys, zs_):
        return pl.ds(pl.multiple_of(64 * ys + 16 * zs_, 16), 16)

    def zj(j):
        return (zh + DZ[j]) % NZH

    def ys_of(way, t):
        return (y - t) % NY if way == 0 else (y + t) % NY

    def next_y(way):
        return at(y_=(y + 1) % NY) if way == 0 else at(y_=(y + NY - 1) % NY)

    def ways(t, j):
        if t < 3:
            return (0, 1)
        return (0,) if j < 2 else (1,)

    def gather(t, j):
        if t == 0 and j > 0:
            block = a_all.at[rows_of(y, zj(j))]
            arrived(block, az_s.at[j], az_r.at[j])
        for way in ways(t, j):
            block = a_all.at[rows_of(ys_of(way, t), zj(j))]
            if t > 0:
                arrived(block, ay_s.at[way, t - 1, j], ay_r.at[way, t - 1, j])
            send(block, block, ay_s.at[way, t, j], ay_r.at[way, t, j], next_y(way))

    arrived(act_in, pair_s.at[0], pair_r.at[0])
    mine, theirs = act_f[c], act_in[...]
    a_all[rows_of(y, zh), :] = jnp.concatenate(
        [jnp.where(c == 0, mine, theirs), jnp.where(c == 0, theirs, mine)], axis=0
    ).astype(bf16)
    own_block = a_all.at[rows_of(y, zh)]
    for r in (1, 3, 2):
        j = DZ.index((NZH - r) % NZH)
        send(own_block, own_block, az_s.at[j], az_r.at[j], at(zh_=(zh + r) % NZH))
    gather(0, 0)

    arrived(pf_in, pair_s.at[1], pair_r.at[1])
    for j in range(2):
        for yd in range(NY):
            mine, theirs = pf[16 * c + 8 * j + yd], pf_in[8 * j + yd]
            q[j, yd] = jnp.concatenate(
                [jnp.where(c == 0, mine, theirs), jnp.where(c == 0, theirs, mine)], axis=0
            ).astype(bf16)
    for r in range(1, NY):
        to = (y + r) % NY
        send(q.at[:, to], qin.at[:, y], gy_s.at[r], gy_r.at[r], at(y_=to))
    qin[:, pl.ds(y, 1)] = q[:, pl.ds(y, 1)]

    z16 = pl.ds(pl.multiple_of(16 * zh, 16), 16)
    holder = c == zh // 2

    def features_z():
        for r in range(1, NY):
            arrived(qin.at[:, (y + NY - r) % NY], gy_s.at[r], gy_r.at[r])
        for j in range(2):
            to = 2 * c + j

            @pl.when(to != zh)
            def _():
                copy(qin.at[j], gf.at[x, :, z16], gz_s.at[j], gz_r.at[zh], at(zh_=to)).start()

            @pl.when(to == zh)
            def _():
                gf[x, :, z16, :] = qin[j]

    def features_x():
        @pl.when(holder)
        def _():
            for r in range(1, NZH):
                src = (zh + NZH - r) % NZH
                rows = pl.ds(pl.multiple_of(16 * src, 16), 16)
                copy(gf.at[x, :, rows], gf.at[x, :, rows], gz_s.at[0], gz_r.at[src], pair).wait_recv()
            for r in range(1, NX):
                copy(gf.at[x], gf.at[x], gx_s.at[r], gx_r.at[r], at(x_=(x + r) % NX)).start()
            copy(gf.at[x], gf.at[x], gd_s.at[0], gd_r.at[0], pair).start()

    def features_pair():
        @pl.when(holder)
        def _():
            for r in range(1, NX):
                block = gf.at[(x + NX - r) % NX]
                copy(block, block, gx_s.at[r], gx_r.at[r], pair).wait_recv()
                copy(block, block, gd_s.at[r], gd_r.at[r], pair).start()

    def features_here():
        @pl.when(jnp.logical_not(holder))
        def _():
            for r in range(NX):
                block = gf.at[(x + NX - r) % NX]
                copy(block, block, gd_s.at[r], gd_r.at[r], pair).wait_recv()

    gather(1, 0)
    features_z()
    gather(0, 1)
    gather(0, 2)
    features_x()
    gather(2, 0)
    gather(1, 1)
    gather(1, 2)
    gather(0, 3)
    features_pair()
    gather(3, 0)
    gather(2, 1)
    gather(2, 2)
    gather(1, 3)
    w_copy.wait()
    arrived(w_in, pair_s.at[2], pair_r.at[2])
    wp[...] = jnp.zeros_like(wp)
    wp[:, 0:WIDE] = jnp.where(c == 0, w_own[...], w_in[...])
    wp[:, 256:256 + WIDE] = jnp.where(c == 0, w_in[...], w_own[...])
    gather(3, 1)
    gather(2, 3)
    gather(3, 2)
    features_here()
    gather(3, 3)

    def features():
        return jnp.concatenate([gf[i].reshape(TOKENS, 128) for i in range(NX)], axis=1)

    def columns(k):
        return slice(CHUNK * k, CHUNK * (k + 1))

    def partial(yd, k, low, count):
        rows = pl.ds(pl.multiple_of(64 * yd + low, 16), count)
        return dyp[rows, columns(k)]

    def reduce_step(t, k):
        for way in range(2):
            if t == 0:
                part = (slice(0, 32),)
                val = partial((y + 4) % NY, k, 32 * way, 32)
            else:
                part = ()
                yd = (y + 4 - t) % NY if way == 0 else (y + NY - 4 + t) % NY
                if t == 1:
                    inc = rb.at[way, 0, k, slice(0, 32)]
                    arrived(inc, rs_s.at[way, 0, k], rs_r.at[way, 0, k])
                    low, high = partial(yd, k, 0, 32), partial(yd, k, 32, 32)
                    if way == 0:
                        low = low + inc[...].astype(f32)
                    else:
                        high = high + inc[...].astype(f32)
                    val = jnp.concatenate([low, high], axis=0)
                else:
                    inc = rb.at[way, t - 1, k]
                    arrived(inc, rs_s.at[way, t - 1, k], rs_r.at[way, t - 1, k])
                    val = partial(yd, k, 0, 64) + inc[...].astype(f32)
            src, dst = sb.at[(way, t, k) + part], rb.at[(way, t, k) + part]
            src[...] = val.astype(bf16)
            send(src, dst, rs_s.at[way, t, k], rs_r.at[way, t, k], next_y(way))

    def reduce_z(k):
        val = partial(y, k, 0, 64)
        for way in range(2):
            inc = rb.at[way, 3, k]
            arrived(inc, rs_s.at[way, 3, k], rs_r.at[way, 3, k])
            val = val + inc[...].astype(f32)
        zs[k] = val
        for r in range(1, NZH):
            to = (zh + r) % NZH
            rows = pl.ds(pl.multiple_of(16 * to, 16), 16)
            send(zs.at[k, rows], zr.at[k, r - 1], rz_s.at[k, r - 1], rz_r.at[k, r - 1], at(zh_=to))

    def reduce_end(k):
        val = zs[k, pl.ds(pl.multiple_of(16 * zh, 16), 16), :]
        for r in range(1, NZH):
            inc = zr.at[k, r - 1]
            arrived(inc, rz_s.at[k, r - 1], rz_r.at[k, r - 1])
            val = val + inc[...]
        fin[0, :, columns(k)] = val[0:8]
        fin[1, :, columns(k)] = val[8:16]

    def product(k):
        dyp[:, columns(k)] = lax.dot_general(
            features(), wp[columns(k), :], (((1,), (1,)), ((), ())), preferred_element_type=f32
        )

    for k in range(NK):
        product(k)
        reduce_step(0, k)

    for j in range(4):
        for way in range(2):
            t = 3 if way in ways(3, j) else 2
            block = a_all.at[rows_of(ys_of(way, t + 1), zj(j))]
            arrived(block, ay_s.at[way, t, j], ay_r.at[way, t, j])

    total = jnp.zeros((8, 128), f32)
    for k in range(NK):
        reduce_step(1, k)
        val = lax.dot_general(
            a_all[:, columns(k)], features(), (((0,), (0,)), ((), ())), preferred_element_type=f32
        )
        raw[0, columns(k), :] = val[:, 0:256]
        raw[1, columns(k), :] = val[:, 256:512]
        send(raw.at[oc, columns(k)], raw_in.at[columns(k)], raw_s.at[k], raw_r.at[k], pair)
        part = jnp.sum((val * val).reshape(CHUNK // 8, 8, 512), axis=0)
        total = total + (part[:, 0:128] + part[:, 128:256] + part[:, 256:384] + part[:, 384:512])

    stages = (
        [pair],
        [at(x_=(x + r) % NX) for r in range(1, NX)],
        [at(y_=(y + r) % NY) for r in range(1, NY)],
        [at(zl_=(zl + r) % NZL) for r in range(1, NZL)],
        [at(zh_=(zh + r) % NZH) for r in range(1, NZH)],
    )
    begin = [sum(len(s) for s in stages[:i]) for i in range(len(stages) + 1)]

    def sum_send(i):
        for n, to in enumerate(stages[i]):
            slot = begin[i] + n
            send(ar_src.at[i], ar_in.at[slot], ar_s.at[slot], ar_r.at[slot], to)

    def sum_wait(i):
        val = ar_src[i]
        for slot in range(begin[i], begin[i + 1]):
            arrived(ar_in.at[slot], ar_s.at[slot], ar_r.at[slot])
            val = val + ar_in[slot]
        ar_src[i + 1] = val

    ar_src[0] = total
    sum_send(0)
    reduce_step(2, 0)
    sum_wait(0)
    sum_send(1)
    reduce_step(2, 1)
    reduce_step(2, 2)
    sum_wait(1)
    sum_send(2)
    reduce_step(2, 3)
    reduce_step(2, 4)
    sum_wait(2)
    sum_send(3)
    reduce_step(3, 0)
    reduce_step(3, 1)
    sum_wait(3)
    sum_send(4)
    reduce_step(3, 2)
    reduce_step(3, 3)
    reduce_step(3, 4)
    reduce_z(0)
    reduce_z(1)
    sum_wait(4)

    sumsq = jnp.sum(ar_src[5])
    rms = jnp.sqrt(jnp.full((8, 128), sumsq, f32) / (float(FF) * float(D)) + 1e-06)
    scale = jnp.minimum(1.0, 1.0 / rms)[0:1, 0:1]
    gdv[own_rows, :] = (raw[c] * scale)[:, :WIDE].astype(bf16)
    out0 = pltpu.make_async_copy(gdv.at[own_rows], gd_ref.at[own_rows], local_sem.at[1])
    out0.start()
    reduce_z(2)
    reduce_z(3)
    for k in range(NK):
        arrived(raw_in.at[columns(k)], raw_s.at[k], raw_r.at[k])
    gdv[other_rows, :] = (raw_in[...] * scale)[:, :WIDE].astype(bf16)
    out1 = pltpu.make_async_copy(gdv.at[other_rows], gd_ref.at[other_rows], local_sem.at[2])
    out1.start()
    reduce_z(4)

    for k in range(NK):
        reduce_end(k)
    send(fin.at[oc], fin_in, pair_s.at[3], pair_r.at[3], pair)
    mine = fin[c]
    arrived(fin_in, pair_s.at[3], pair_r.at[3])
    theirs = fin_in[...]
    gp_ref[:, 0:HALF] = (jnp.where(c == 0, mine, theirs) * slope[0]).astype(bf16)
    gp_ref[:, HALF:2 * HALF] = (jnp.where(c == 0, theirs, mine) * slope[1]).astype(bf16)

    for cp in later:
        cp.wait_send()
    for j in range(2):
        to = 2 * c + j

        @pl.when(to != zh)
        def _():
            copy(qin.at[j], gf.at[x, :, z16], gz_s.at[j], gz_r.at[zh], at(zh_=to)).wait_send()

    @pl.when(holder)
    def _():
        for r in range(1, NX):
            copy(gf.at[x], gf.at[x], gx_s.at[r], gx_r.at[r], pair).wait_send()
        for r in range(NX):
            copy(gf.at[x], gf.at[x], gd_s.at[r], gd_r.at[r], pair).wait_send()

    out0.wait()
    out1.wait()


def local(hidden_pre, grad_out, w_down):
    dma = pltpu.SemaphoreType.DMA
    vmem = pltpu.VMEM
    n_sum = 1 + (NX - 1) + (NY - 1) + (NZL - 1) + (NZH - 1)
    sems = [
        (3,), (4,), (4,), (NK,), (NK,), (NY,), (NY,), (2,), (NZH,), (NX,), (NX,),
        (NX,), (NX,), (2, 4, 4), (2, 4, 4), (4,), (4,), (2, 4, NK), (2, 4, NK),
        (NK, 3), (NK, 3), (n_sum,), (n_sum,),
    ]
    return pl.pallas_call(
        kernel,
        out_shape=(
            jax.ShapeDtypeStruct(hidden_pre.shape, bf16),
            jax.ShapeDtypeStruct(w_down.shape, bf16),
        ),
        in_specs=[
            pl.BlockSpec(memory_space=pltpu.VMEM),
            pl.BlockSpec(memory_space=pltpu.VMEM),
            pl.BlockSpec(memory_space=pl.ANY),
        ],
        out_specs=(
            pl.BlockSpec(memory_space=pltpu.VMEM),
            pl.BlockSpec(memory_space=pl.ANY),
        ),
        scratch_shapes=[
            vmem((2, 8, HALF), f32),
            vmem((2, 8, HALF), f32),
            vmem((8, HALF), f32),
            vmem((NZH * NY, 8, 128), f32),
            vmem((16, 8, 128), f32),
            vmem((2, NY, 16, 128), bf16),
            vmem((2, NY, 16, 128), bf16),
            vmem((NX, NY, 64, 128), bf16),
            vmem((TOKENS, HALF), bf16),
            vmem((HALF, WIDE), bf16),
            vmem((HALF, WIDE), bf16),
            vmem((HALF, 512), bf16),
            vmem((TOKENS, HALF), f32),
            vmem((2, 4, NK, 64, CHUNK), bf16),
            vmem((2, 4, NK, 64, CHUNK), bf16),
            vmem((NK, 64, CHUNK), f32),
            vmem((NK, 3, 16, CHUNK), f32),
            vmem((2, 8, HALF), f32),
            vmem((8, HALF), f32),
            vmem((2, HALF, 256), f32),
            vmem((HALF, 256), f32),
            vmem((2 * HALF, WIDE), bf16),
            vmem((6, 8, 128), f32),
            vmem((n_sum, 8, 128), f32),
        ] + [dma(s) for s in sems],
        compiler_params=pltpu.CompilerParams(
            collective_id=0, has_side_effects=True, vmem_limit_bytes=50 * 1024 * 1024
        ),
        cost_estimate=pl.CostEstimate(
            flops=4 * TOKENS * 2 * HALF * WIDE, bytes_accessed=6 << 20, transcendentals=0
        ),
    )(hidden_pre, grad_out, w_down)


def solution(mesh):
    placed = (P("dp", "mp"), P("dp", None), P("mp", "dp"))
    return jax.shard_map(
        local, mesh=mesh, in_specs=placed, out_specs=(P("dp", "mp"), P("mp", "dp")), check_vma=False
    )
```

time: 302 us -> 90.1 us (0.30); the launches traced: 298 us -> 90 us
  blocking collectives: 144 us -> 0 us
  waiting for transfers between devices: 125 us -> 0 us
  Pallas kernels: 0 us -> 85.6 us
  between operations: 14.8 us -> 0.68 us
  matrix products: 7.99 us -> 0 us
  other arithmetic: 4.4 us -> 0 us
    psum x1 -> x0, blocking collectives: 107 us -> none  [local(): sumsq = lax.psum(jnp.sum(raw * raw), ('mp', 'dp'))]
    pallas_call x0 -> x1, Pallas kernels: none -> 85.6 us  [local(): pl.pallas_call(kernel, out_shape=(jax.ShapeDtypeStruct(hidden_pre.shape,...]
    all_gather x1 -> x0, waiting for transfers between devices: 66.9 us -> none  [local(): hidden_all = lax.all_gather(hidden_pre, 'dp', axis=0, tiled=True)]
    reduce_scatter x1 -> x0, waiting for transfers between devices: 57.4 us -> none  [local(): lax.psum_scatter(row_products(dy_cols, w_down), 'dp', scatter_dimension=0...]
    all_to_all x1 -> x0, blocking collectives: 37.1 us -> none  [local(): lax.all_to_all(grad_out, 'dp', split_axis=1, concat_axis=0, tiled=True)]
    dot_general x2 -> x0, matrix products: 7.99 us -> none  [the longest x1 4.83 us: weight_terms(): lax.dot_general(act, dy_rows, (((0,), (0,)), ((), ())), preferred_element...]
    convert_element_type x2 -> x0, other arithmetic: 4.4 us -> none  [the longest x1 2.85 us: local(): grad_down = (raw * jnp.minimum(1.0, 1.0 / rms)).astype(jnp.bfloat16)]
  transfers between devices with their start and end apart: 2 -> 0, of which waited for: 2 -> 0; matrix products, arithmetic and copies ran while one was open for 4% -> 0% of each run, Pallas kernels for 0% -> 0%
where the time goes in v1:
time: 90.1 us; the launch traced here: 90 us
  Pallas kernels  85.6 us (95%)
  local copies, waits for them, and re-layouts  3.65 us (4%)
    pallas_call x1, Pallas kernels, local(): pl.pallas_call(kernel, out_shape=(jax.ShapeDtypeStruct(hidden_pre.shape,...  85.6 us
    unnamed x6, local copies, waits for them, and re-layouts  2.24 us

profile of v1, /device:TPU:1, one launch (start us, length us, event | category | flops | bytes accessed | tf_op | source)
XLA Modules:
  0.0 90.0 jit_solution(5010238208761132040)
XLA Ops:
  0.6 0.0 copy-start
  0.6 0.0 copy-start.1
  0.6 1.6 %copy.5.w_ref = bf16[2560,232]{1,0:T(8,128)(2,1)S(1)} copy(bf16[2560,232]{0,1:T(8,128)(2,1)} %param.5) | data formatting | bytes 2375680 | tf_op args[2]
  2.3 0.0 copy-done
  2.3 0.0 copy-done.1
  2.3 85.6 %shard_map.50 = (bf16[8,2560]{1,0:T(8,128)(2,1)S(1)}, bf16[2560,232]{1,0:T(8,128)(2,1)S(1)}) custom-call(bf16[8,2560]{1,0:T(8,128)(2,1)S(1)} %copy-done.1, bf16[8,14848]{1,0:T(8,128)(2,1)S(1)} %copy-done, bf16[2560,232]{1,0:T(8,128)(2,1)S(1)} %copy.5.w_ref), custom_call_target="tpu_custom_call" | custom-call | flops 1216348160 | bytes 6291456 | tf_op jit(solution)/shard_map/pallas_call | solution.py:412
  87.9 1.4 %copy.6 = bf16[2560,232]{0,1:T(8,128)(2,1)} copy(bf16[2560,232]{1,0:T(8,128)(2,1)S(1)} %get-tuple-element.3) | data formatting | bytes 2375680 | tf_op jit(solution)/shard_map/pallas_call | solution.py:412
  89.3 0.6 copy.8
Async XLA Ops:
  0.6 1.6 %copy-start = (bf16[8,14848]{1,0:T(8,128)(2,1)S(1)}, bf16[8,14848]{1,0:T(8,128)(2,1)}, u32[]{:S(2)}) copy-start(bf16[8,14848]{1,0:T(8,128)(2,1)} %g_ref.1) | copy-start | bytes 712708
  0.6 1.6 %copy-start.1 = (bf16[8,2560]{1,0:T(8,128)(2,1)S(1)}, bf16[8,2560]{1,0:T(8,128)(2,1)}, u32[]{:S(2)}) copy-start(bf16[8,2560]{1,0:T(8,128)(2,1)} %h_ref.1) | copy-start | bytes 122884

commit v2 on v1

v2 whole, which is shorter than its diff:
```python
import functools

import jax
import jax.numpy as jnp
from jax import lax
from jax.experimental import pallas as pl
from jax.experimental.pallas import tpu as pltpu
from jax.sharding import PartitionSpec as P

root_half = 0.7071067811865476
inv_root_tau = 0.3989422804014327

f32, bf16 = jnp.float32, jnp.bfloat16
MESH = pl.DeviceIdType.MESH

NX, NZL, NY, NZH = 4, 3, 8, 4
D, FF, TOKENS = 14848, 30720, 512
WIDE = 232
HALF = 1280
CHUNK = 256
NK = HALF // CHUNK
DZ = (0, 1, 3, 2, 2)
PIECE = (slice(0, HALF),) * 3 + (slice(0, HALF // 2), slice(HALF // 2, HALF))


def gelu_value(value):
    return 0.5 * value * (1.0 + lax.erf(value * root_half))


def gelu_slope(value):
    return (
        0.5 * (1.0 + lax.erf(value * root_half))
        + value * jnp.exp(-0.5 * value * value) * inv_root_tau
    )


def kernel(
    h_ref, g_ref, w_ref, gp_ref, gd_ref,
    slope, act_f, act_in, pf, pf_in, q, qin, gf, gt, a_all, w_own, w_in, wp,
    dyp, sb, rb, zs, z1, z2, z1_in, z2_in, fin, fin_in, raw, raw_in, gdv, ar_src, ar_in,
    local_sem, pair_s, pair_r, raw_s, raw_r, gy_s, gy_r, gz_s, gz_r, gx_s, gx_r,
    gd_s, gd_r, ay_s, ay_r, az_s, az_r, rs_s, rs_r, rz_s, rz_r, fin_s, fin_r, ar_s, ar_r,
):
    mp, dp = lax.axis_index("mp"), lax.axis_index("dp")
    x, zl = mp % NX, mp // NX
    c, y, zh = dp % 2, (dp // 2) % NY, dp // (2 * NY)
    oc = 1 - c

    def at(x_=None, zl_=None, c_=None, y_=None, zh_=None):
        x_ = x if x_ is None else x_
        zl_ = zl if zl_ is None else zl_
        c_ = c if c_ is None else c_
        y_ = y if y_ is None else y_
        zh_ = zh if zh_ is None else zh_
        return (zl_ * NX + x_, (zh_ * NY + y_) * 2 + c_)

    pair = at(c_=oc)
    later = []

    def copy(src, dst, ss, rs, to):
        return pltpu.make_async_remote_copy(
            src_ref=src, dst_ref=dst, send_sem=ss, recv_sem=rs, device_id=to, device_id_type=MESH
        )

    def send(src, dst, ss, rs, to):
        cp = copy(src, dst, ss, rs, to)
        cp.start()
        later.append(cp)

    def arrived(dst, ss, rs):
        copy(dst, dst, ss, rs, pair).wait_recv()

    barrier = pltpu.get_barrier_semaphore()
    peers = [pair]
    peers += [at(x_=(x + r) % NX) for r in range(1, NX)]
    peers += [at(y_=(y + r) % NY) for r in range(1, NY)]
    depth = NZL * NZH
    along_z = [(NZL * zh + zl + r) % depth for r in range(1, depth)]
    along_z = [at(zl_=p % NZL, zh_=p // NZL) for p in along_z]
    peers += along_z
    for peer in peers:
        pl.semaphore_signal(barrier, inc=1, device_id=peer, device_id_type=MESH)

    own_cols = pl.ds(pl.multiple_of(HALF * c, 128), HALF)
    other_cols = pl.ds(pl.multiple_of(HALF * oc, 128), HALF)
    w_copy = pltpu.make_async_copy(w_ref.at[:, own_cols], w_own, local_sem.at[0])
    w_copy.start()

    tile = x % 2
    first = WIDE * (x // 2) + 128 * tile
    lanes = lax.broadcasted_iota(jnp.int32, (8, 128), 1)
    keep = lanes < 128 - (256 - WIDE) * tile
    for d in range(NZH * NY):
        if d < NZH * NY - 1:
            off = 2 * WIDE * d + first
            start, width = (off // 128) * 128, 256
            window = g_ref[:, pl.ds(pl.multiple_of(start, 128), width)]
        else:
            off = 2 * WIDE * d + first
            start, width = D - 512, 512
            window = g_ref[:, start:start + width]
        rolled = pltpu.roll(window.astype(f32), width - (off - start), axis=1)
        pf[d] = jnp.where(keep, rolled[:, :128], 0.0)

    pl.semaphore_wait(barrier, len(peers))
    send(pf.at[pl.ds(16 * oc, 16)], pf_in, pair_s.at[1], pair_r.at[1], pair)

    for half in range(2):
        hidden = h_ref[:, HALF * half:HALF * (half + 1)].astype(f32)
        act_f[half] = gelu_value(hidden).astype(bf16).astype(f32)

    send(act_f.at[oc], act_in, pair_s.at[0], pair_r.at[0], pair)

    def rows_of(ys, zs_):
        return pl.ds(pl.multiple_of(64 * ys + 16 * zs_, 16), 16)

    def zj(j):
        return (zh + DZ[j]) % NZH

    def ys_of(way, t):
        return (y - t) % NY if way == 0 else (y + t) % NY

    def next_y(way):
        return at(y_=(y + 1) % NY) if way == 0 else at(y_=(y + NY - 1) % NY)

    def ways(t, j):
        if t < 3:
            return (0, 1)
        return (0,) if j < 2 else (1,)

    def piece(ys, j):
        return a_all.at[rows_of(ys, zj(j)), PIECE[j]]

    def gather(t, j):
        if t == 0 and j > 2:
            arrived(piece(y, j), az_s.at[j], az_r.at[j])
        for way in ways(t, j):
            block = piece(ys_of(way, t), j)
            if t > 0:
                arrived(block, ay_s.at[way, t - 1, j], ay_r.at[way, t - 1, j])
            send(block, block, ay_s.at[way, t, j], ay_r.at[way, t, j], next_y(way))

    up, down = at(zh_=(zh + 1) % NZH), at(zh_=(zh + NZH - 1) % NZH)

    def relay(i):
        j, to, half = ((2, up, 3), (1, down, 4))[i]
        arrived(piece(y, j), az_s.at[j], az_r.at[j])
        block = a_all.at[rows_of(y, zj(j)), PIECE[half]]
        send(block, block, az_s.at[half], az_r.at[half], to)

    arrived(pf_in, pair_s.at[1], pair_r.at[1])
    for j in range(2):
        for yd in range(NY):
            mine, theirs = pf[16 * c + 8 * j + yd], pf_in[8 * j + yd]
            q[j, yd] = jnp.concatenate(
                [jnp.where(c == 0, mine, theirs), jnp.where(c == 0, theirs, mine)], axis=0
            ).astype(bf16)
    for r in range(1, NY):
        to = (y + r) % NY
        send(q.at[:, to], qin.at[:, y], gy_s.at[r], gy_r.at[r], at(y_=to))
    qin[:, pl.ds(y, 1)] = q[:, pl.ds(y, 1)]

    arrived(act_in, pair_s.at[0], pair_r.at[0])
    mine, theirs = act_f[c], act_in[...]
    a_all[rows_of(y, zh), :] = jnp.concatenate(
        [jnp.where(c == 0, mine, theirs), jnp.where(c == 0, theirs, mine)], axis=0
    ).astype(bf16)
    own_block = a_all.at[rows_of(y, zh)]
    send(own_block, own_block, az_s.at[2], az_r.at[2], up)
    send(own_block, own_block, az_s.at[1], az_r.at[1], down)
    gather(0, 0)

    z16 = pl.ds(pl.multiple_of(16 * zh, 16), 16)
    holder = c == zh // 2

    def token_rows(dz):
        return pl.ds(pl.multiple_of(16 * ((zh + dz) % NZH), 16), 16)

    near, far = 2 * c + 1 - zh % 2, 2 * c + zh % 2
    near_at, far_at = at(zh_=near), at(zh_=far, zl_=(zl + 1) % NZL)

    def features_z():
        for r in range(1, NY):
            arrived(qin.at[:, (y + NY - r) % NY], gy_s.at[r], gy_r.at[r])
        send(qin.at[1 - zh % 2], gf.at[x, :, z16], gz_s.at[0], gz_r.at[zh], near_at)

        @pl.when(jnp.logical_not(holder))
        def _():
            copy(qin.at[zh % 2], gf.at[x, :, z16], gz_s.at[1], gz_r.at[zh], far_at).start()

        @pl.when(holder)
        def _():
            gf[x, :, z16, :] = qin[zh % 2]

    def features_x(dz):
        @pl.when(holder)
        def _():
            block = gf.at[x, :, token_rows(dz)]
            if dz > 0:
                copy(block, block, gz_s.at[0], gz_r.at[(zh + dz) % NZH], pair).wait_recv()
            for r in range(1, NX):
                copy(block, block, gx_s.at[r, dz], gx_r.at[r, dz], at(x_=(x + r) % NX)).start()
            copy(block, block, gd_s.at[0, dz], gd_r.at[0, dz], pair).start()

    def features_pair(dz):
        @pl.when(holder)
        def _():
            for r in range(1, NX):
                block = gf.at[(x + NX - r) % NX, :, token_rows(dz)]
                copy(block, block, gx_s.at[r, dz], gx_r.at[r, dz], pair).wait_recv()
                copy(block, block, gd_s.at[r, dz], gd_r.at[r, dz], pair).start()

    def features_here():
        @pl.when(jnp.logical_not(holder))
        def _():
            for dz in range(NZH):
                for r in range(NX):
                    block = gf.at[(x + NX - r) % NX, :, token_rows(dz)]
                    copy(block, block, gd_s.at[r, dz], gd_r.at[r, dz], pair).wait_recv()

    def weights():
        w_copy.wait()
        arrived(w_in, pair_s.at[2], pair_r.at[2])
        for b in range(2):
            wp[256 * b:256 * b + WIDE, :] = jnp.where(c == b, w_own[...], w_in[...])
            wp[256 * b + WIDE:256 * (b + 1), :] = jnp.zeros((256 - WIDE, HALF), bf16)

    def features():
        return jnp.concatenate([gf[i].reshape(TOKENS, 128) for i in range(NX)], axis=1)

    def turned():
        for i in range(NX):
            gt[128 * i:128 * (i + 1), :] = gf[i].reshape(TOKENS, 128).astype(f32).T.astype(bf16)

    def columns(k):
        return slice(CHUNK * k, CHUNK * (k + 1))

    def partial(yd, k, low, count):
        rows = pl.ds(pl.multiple_of(64 * yd + low, 16), count)
        return dyp[rows, columns(k)]

    def reduce_step(t, k):
        for way in range(2):
            if t == 0:
                part = (slice(0, 32),)
                val = partial((y + 4) % NY, k, 32 * way, 32)
            else:
                part = ()
                yd = (y + 4 - t) % NY if way == 0 else (y + NY - 4 + t) % NY
                if t == 1:
                    inc = rb.at[way, 0, k, slice(0, 32)]
                    arrived(inc, rs_s.at[way, 0, k], rs_r.at[way, 0, k])
                    low, high = partial(yd, k, 0, 32), partial(yd, k, 32, 32)
                    if way == 0:
                        low = low + inc[...].astype(f32)
                    else:
                        high = high + inc[...].astype(f32)
                    val = jnp.concatenate([low, high], axis=0)
                else:
                    inc = rb.at[way, t - 1, k]
                    arrived(inc, rs_s.at[way, t - 1, k], rs_r.at[way, t - 1, k])
                    val = partial(yd, k, 0, 64) + inc[...].astype(f32)
            src, dst = sb.at[(way, t, k) + part], rb.at[(way, t, k) + part]
            src[...] = val.astype(bf16)
            send(src, dst, rs_s.at[way, t, k], rs_r.at[way, t, k], next_y(way))

    def z_rows(dz):
        return pl.ds(pl.multiple_of(16 * ((zh + dz) % NZH), 16), 16)

    def reduce_z(k):
        val = partial(y, k, 0, 64)
        for way in range(2):
            inc = rb.at[way, 3, k]
            arrived(inc, rs_s.at[way, 3, k], rs_r.at[way, 3, k])
            val = val + inc[...].astype(f32)
        zs[k] = val
        for way, to in ((0, up), (1, down)):
            z1[k, way] = zs[k, z_rows(2), 128 * way:128 * (way + 1)]
            send(z1.at[k, way], z1_in.at[k, way], rz_s.at[k, way], rz_r.at[k, way], to)

    def reduce_z2(k):
        for way, to in ((0, up), (1, down)):
            arrived(z1_in.at[k, way], rz_s.at[k, way], rz_r.at[k, way])
            val = zs[k, z_rows(1 if way == 0 else 3), :]
            inc = z1_in[k, way]
            parts = [val[:, :128], val[:, 128:]]
            parts[way] = parts[way] + inc
            z2[k, way] = jnp.concatenate(parts, axis=1)
            send(z2.at[k, way], z2_in.at[k, way], rz_s.at[k, 2 + way], rz_r.at[k, 2 + way], to)

    def reduce_end(k):
        val = zs[k, z_rows(0), :]
        for way in range(2):
            arrived(z2_in.at[k, way], rz_s.at[k, 2 + way], rz_r.at[k, 2 + way])
            val = val + z2_in[k, way]
        fin[k, 0] = val[0:8]
        fin[k, 1] = val[8:16]
        send(fin.at[k, oc], fin_in.at[k], fin_s.at[k], fin_r.at[k], pair)

    def product(k):
        dyp[:, columns(k)] = lax.dot_general(
            features(), wp[:, columns(k)], (((1,), (0,)), ((), ())), preferred_element_type=f32
        )

    def gathered():
        for j in range(len(DZ)):
            for way in range(2):
                t = 3 if way in ways(3, j) else 2
                arrived(piece(ys_of(way, t + 1), j), ay_s.at[way, t, j], ay_r.at[way, t, j])

    def weight_grad(k):
        val = lax.dot_general(
            gt[...], a_all[:, columns(k)], (((1,), (0,)), ((), ())), preferred_element_type=f32
        )
        for b in range(2):
            raw[b, :, columns(k)] = val[256 * b:256 * b + WIDE]
        send(
            raw.at[oc, :, columns(k)], raw_in.at[:, columns(k)], raw_s.at[k], raw_r.at[k], pair
        )
        part = jnp.sum((val * val).reshape(512 // 8, 8, CHUNK), axis=0)
        part = part[:, 0:128] + part[:, 128:256]
        ar_src[0] = part if k == 0 else ar_src[0] + part

    stages = (
        [pair],
        [at(x_=(x + r) % NX) for r in range(1, NX)],
        [at(y_=(y + r) % NY) for r in range(1, NY)],
        along_z,
    )
    begin = [sum(len(s) for s in stages[:i]) for i in range(len(stages) + 1)]

    def sum_send(i):
        for n, to in enumerate(stages[i]):
            slot = begin[i] + n
            send(ar_src.at[i], ar_in.at[slot], ar_s.at[slot], ar_r.at[slot], to)

    def sum_wait(i):
        val = ar_src[i]
        for slot in range(begin[i], begin[i + 1]):
            arrived(ar_in.at[slot], ar_s.at[slot], ar_r.at[slot])
            val = val + ar_in[slot]
        ar_src[i + 1] = val

    def scaled():
        sumsq = jnp.sum(ar_src[4])
        rms = jnp.sqrt(jnp.full((8, 128), sumsq, f32) / (float(FF) * float(D)) + 1e-06)
        scale = jnp.minimum(1.0, 1.0 / rms)[0:1, 0:1]
        gdv[:, own_cols] = (raw[c] * scale).astype(bf16)
        out0 = pltpu.make_async_copy(gdv.at[:, own_cols], gd_ref.at[:, own_cols], local_sem.at[1])
        out0.start()
        for k in range(NK):
            arrived(raw_in.at[:, columns(k)], raw_s.at[k], raw_r.at[k])
        gdv[:, other_cols] = (raw_in[...] * scale).astype(bf16)
        out1 = pltpu.make_async_copy(
            gdv.at[:, other_cols], gd_ref.at[:, other_cols], local_sem.at[2]
        )
        out1.start()
        return out0, out1

    def slopes():
        for half in range(2):
            slope[half] = gelu_slope(h_ref[:, HALF * half:HALF * (half + 1)].astype(f32))

    send(w_ref.at[:, other_cols], w_in, pair_s.at[2], pair_r.at[2], pair)
    slopes()
    weights()
    gather(1, 0)
    features_z()
    features_x(0)
    relay(0)
    relay(1)
    gather(0, 2)
    gather(0, 1)
    gather(2, 0)
    gather(1, 2)
    features_pair(0)
    features_x(1)
    features_x(3)
    gather(1, 1)
    gather(3, 0)
    gather(0, 3)
    features_x(2)
    gather(0, 4)
    gather(2, 2)
    gather(2, 1)
    features_pair(1)
    gather(1, 3)
    features_pair(3)
    gather(1, 4)
    features_pair(2)
    gather(3, 2)
    gather(3, 1)
    features_here()
    gather(2, 3)
    turned()
    gather(2, 4)
    product(0)
    reduce_step(0, 0)
    product(1)
    reduce_step(0, 1)
    product(2)
    reduce_step(0, 2)
    product(3)
    reduce_step(0, 3)
    product(4)
    reduce_step(0, 4)
    gather(3, 3)
    gather(3, 4)
    reduce_step(1, 0)
    reduce_step(1, 1)
    reduce_step(1, 2)
    reduce_step(1, 3)
    reduce_step(1, 4)
    gathered()
    weight_grad(0)
    weight_grad(1)
    reduce_step(2, 0)
    weight_grad(2)
    weight_grad(3)
    weight_grad(4)
    sum_send(0)
    reduce_step(2, 1)
    reduce_step(2, 2)
    sum_wait(0)
    sum_send(1)
    reduce_step(2, 3)
    reduce_step(2, 4)
    reduce_step(3, 0)
    reduce_step(3, 1)
    sum_wait(1)
    sum_send(2)
    reduce_step(3, 2)
    reduce_step(3, 3)
    reduce_step(3, 4)
    reduce_z(0)
    reduce_z(1)
    reduce_z(2)
    sum_wait(2)
    sum_send(3)
    reduce_z(3)
    reduce_z(4)
    reduce_z2(0)
    reduce_z2(1)
    reduce_z2(2)
    reduce_z2(3)
    reduce_z2(4)
    sum_wait(3)
    reduce_end(0)
    outs = scaled()
    reduce_end(1)
    reduce_end(2)
    reduce_end(3)
    reduce_end(4)

    for k in range(NK):
        arrived(fin_in.at[k], fin_s.at[k], fin_r.at[k])
        mine, theirs = fin[k, c], fin_in[k]
        for half in range(2):
            cols = slice(HALF * half + CHUNK * k, HALF * half + CHUNK * (k + 1))
            gp_ref[:, cols] = (jnp.where(c == half, mine, theirs) * slope[half, :, columns(k)]).astype(bf16)

    for cp in later:
        cp.wait_send()
    @pl.when(jnp.logical_not(holder))
    def _():
        copy(qin.at[0], gf.at[x, :, z16], gz_s.at[1], gz_r.at[zh], pair).wait_send()

    @pl.when(holder)
    def _():
        for dz in range(NZH):
            block = gf.at[x, :, token_rows(dz)]
            for r in range(NX):
                if r > 0:
                    copy(block, block, gx_s.at[r, dz], gx_r.at[r, dz], pair).wait_send()
                copy(block, block, gd_s.at[r, dz], gd_r.at[r, dz], pair).wait_send()

    for out in outs:
        out.wait()


def local(hidden_pre, grad_out, w_down):
    dma = pltpu.SemaphoreType.DMA
    vmem = pltpu.VMEM
    n_sum = 1 + (NX - 1) + (NY - 1) + (NZL * NZH - 1)
    sems = [
        (3,), (3,), (3,), (NK,), (NK,), (NY,), (NY,), (2,), (NZH,), (NX, NZH), (NX, NZH),
        (NX, NZH), (NX, NZH), (2, 4, 5), (2, 4, 5), (5,), (5,), (2, 4, NK), (2, 4, NK),
        (NK, 4), (NK, 4), (NK,), (NK,), (n_sum,), (n_sum,),
    ]
    grad_pre, grad_down = pl.pallas_call(
        kernel,
        out_shape=(
            jax.ShapeDtypeStruct(hidden_pre.shape, bf16),
            jax.ShapeDtypeStruct(w_down.T.shape, bf16),
        ),
        in_specs=[
            pl.BlockSpec(memory_space=pltpu.VMEM),
            pl.BlockSpec(memory_space=pltpu.VMEM),
            pl.BlockSpec(memory_space=pl.ANY),
        ],
        out_specs=(
            pl.BlockSpec(memory_space=pltpu.VMEM),
            pl.BlockSpec(memory_space=pl.ANY),
        ),
        scratch_shapes=[
            vmem((2, 8, HALF), f32),
            vmem((2, 8, HALF), f32),
            vmem((8, HALF), f32),
            vmem((NZH * NY, 8, 128), f32),
            vmem((16, 8, 128), f32),
            vmem((2, NY, 16, 128), bf16),
            vmem((2, NY, 16, 128), bf16),
            vmem((NX, NY, 64, 128), bf16),
            vmem((512, TOKENS), bf16),
            vmem((TOKENS, HALF), bf16),
            vmem((WIDE, HALF), bf16),
            vmem((WIDE, HALF), bf16),
            vmem((512, HALF), bf16),
            vmem((TOKENS, HALF), f32),
            vmem((2, 4, NK, 64, CHUNK), bf16),
            vmem((2, 4, NK, 64, CHUNK), bf16),
            vmem((NK, 64, CHUNK), f32),
            vmem((NK, 2, 16, 128), f32),
            vmem((NK, 2, 16, CHUNK), f32),
            vmem((NK, 2, 16, 128), f32),
            vmem((NK, 2, 16, CHUNK), f32),
            vmem((NK, 2, 8, CHUNK), f32),
            vmem((NK, 8, CHUNK), f32),
            vmem((2, WIDE, HALF), f32),
            vmem((WIDE, HALF), f32),
            vmem((WIDE, 2 * HALF), bf16),
            vmem((5, 8, 128), f32),
            vmem((n_sum, 8, 128), f32),
        ] + [dma(s) for s in sems],
        compiler_params=pltpu.CompilerParams(
            collective_id=0, has_side_effects=True, vmem_limit_bytes=50 * 1024 * 1024
        ),
        cost_estimate=pl.CostEstimate(
            flops=4 * TOKENS * 2 * HALF * WIDE, bytes_accessed=6 << 20, transcendentals=0
        ),
    )(hidden_pre, grad_out, w_down.T)
    return grad_pre, grad_down.T


def solution(mesh):
    placed = (P("dp", "mp"), P("dp", None), P("mp", "dp"))
    return jax.shard_map(
        local, mesh=mesh, in_specs=placed, out_specs=(P("dp", "mp"), P("mp", "dp")), check_vma=False
    )
```

time: 90.1 us -> 78.5 us (0.87)
  Pallas kernels: 85.6 us -> 73 us
  local copies, waits for them, and re-layouts: 3.65 us -> 4.62 us
    pallas_call x1, Pallas kernels: 85.6 us -> 73 us  [local(): pl.pallas_call(kernel, out_shape=(jax.ShapeDtypeStruct(hidden_pre.shape,...]
    unnamed x6 -> x8, local copies, waits for them, and re-layouts: 2.24 us -> 4.62 us
    pallas_call x1 -> x0, local copies, waits for them, and re-layouts: 1.41 us -> none  [local(): pl.pallas_call(kernel, out_shape=(jax.ShapeDtypeStruct(hidden_pre.shape,...]
where the time goes in v2:
time: 78.5 us; the launch traced here: 78.3 us
  Pallas kernels  73 us (93%)
  local copies, waits for them, and re-layouts  4.62 us (6%)
    pallas_call x1, Pallas kernels, local(): pl.pallas_call(kernel, out_shape=(jax.ShapeDtypeStruct(hidden_pre.shape,...  73 us
    unnamed x8, local copies, waits for them, and re-layouts  4.62 us

profile of v2, /device:TPU:1, one launch (start us, length us, event | category | flops | bytes accessed | tf_op | source)
XLA Modules:
  0.0 78.3 jit_solution(14277335518420961573)
XLA Ops:
  0.6 0.0 copy-start
  0.6 1.3 %copy-done = bf16[2560,232]{0,1:T(8,128)(2,1)S(1)} copy-done((bf16[2560,232]{0,1:T(8,128)(2,1)S(1)}, bf16[2560,232]{0,1:T(8,128)(2,1)}, u32[]{:S(2)}) %copy-start) | copy-done | bytes 1187864
  1.9 0.0 copy-start.1
  1.9 0.9 %copy-done.1 = bf16[8,14848]{1,0:T(8,128)(2,1)S(1)} copy-done((bf16[8,14848]{1,0:T(8,128)(2,1)S(1)}, bf16[8,14848]{1,0:T(8,128)(2,1)}, u32[]{:S(2)}) %copy-start.1) | copy-done | bytes 237592
  2.8 0.0 copy-start.2
  2.8 0.8 copy-done.2
  3.6 73.0 %shard_map.50 = (bf16[8,2560]{1,0:T(8,128)(2,1)S(1)}, bf16[232,2560]{1,0:T(8,128)(2,1)S(1)}) custom-call(bf16[8,2560]{1,0:T(8,128)(2,1)S(1)} %copy-done.2, bf16[8,14848]{1,0:T(8,128)(2,1)S(1)} %copy-done.1, bf16[232,2560]{1,0:T(8,128)(2,1)S(1)} %bitcast.3), custom_call_target="tpu_custom_call" | custom-call | flops 1216348160 | bytes 6291456 | tf_op jit(solution)/shard_map/pallas_call | solution.py:490
  76.6 0.6 copy.7
  77.2 1.0 %copy.8 = bf16[2560,232]{0,1:T(8,128)(2,1)} copy(bf16[2560,232]{0,1:T(8,128)(2,1)S(1)} %bitcast.2) | data formatting | bytes 2375680
Async XLA Ops:
  0.6 1.3 %copy-start = (bf16[2560,232]{0,1:T(8,128)(2,1)S(1)}, bf16[2560,232]{0,1:T(8,128)(2,1)}, u32[]{:S(2)}) copy-start(bf16[2560,232]{0,1:T(8,128)(2,1)} %param.5) | copy-start | bytes 3563524
  1.9 0.9 %copy-start.1 = (bf16[8,14848]{1,0:T(8,128)(2,1)S(1)}, bf16[8,14848]{1,0:T(8,128)(2,1)}, u32[]{:S(2)}) copy-start(bf16[8,14848]{1,0:T(8,128)(2,1)} %g_ref.1) | copy-start | bytes 712708
  2.8 0.8 copy-start.2

commit v3 on v2

--- a/solution.py
+++ b/solution.py
@@ -35,8 +35,8 @@
 
 
 def kernel(
-    h_ref, g_ref, w_ref, gp_ref, gd_ref,
-    slope, act_f, act_in, pf, pf_in, q, qin, gf, gt, a_all, w_own, w_in, wp,
+    h_hbm, g_hbm, w_ref, gp_ref, gd_ref,
+    h_ref, g_ref, slope, act_f, act_in, pf, pf_in, q, qin, gf, gt, a_all, w_own, w_in, wp,
     dyp, sb, rb, zs, z1, z2, z1_in, z2_in, fin, fin_in, raw, raw_in, gdv, ar_src, ar_in,
     local_sem, pair_s, pair_r, raw_s, raw_r, gy_s, gy_r, gz_s, gz_r, gx_s, gx_r,
     gd_s, gd_r, ay_s, ay_r, az_s, az_r, rs_s, rs_r, rz_s, rz_r, fin_s, fin_r, ar_s, ar_r,
@@ -70,14 +70,20 @@
     def arrived(dst, ss, rs):
         copy(dst, dst, ss, rs, pair).wait_recv()
 
+    g_copy = pltpu.make_async_copy(g_hbm, g_ref, local_sem.at[3])
+    h_copy = pltpu.make_async_copy(h_hbm, h_ref, local_sem.at[4])
+    g_copy.start()
+    h_copy.start()
     barrier = pltpu.get_barrier_semaphore()
-    peers = [pair]
-    peers += [at(x_=(x + r) % NX) for r in range(1, NX)]
-    peers += [at(y_=(y + r) % NY) for r in range(1, NY)]
     depth = NZL * NZH
     along_z = [(NZL * zh + zl + r) % depth for r in range(1, depth)]
     along_z = [at(zl_=p % NZL, zh_=p // NZL) for p in along_z]
-    peers += along_z
+    along_y = [at(y_=(y + r) % NY) for r in range(1, NY)]
+    along_x = [at(x_=(x + r) % NX) for r in range(1, NX)]
+    peers = [along_z[r - 1] for r in (6, 5, 7, 4, 8, 3, 9)]
+    peers += [along_y[r - 1] for r in (4, 3, 5, 2, 6)]
+    peers += [along_z[r - 1] for r in (2, 10)] + [along_x[1]]
+    peers += [along_y[0], along_y[6], along_x[0], along_x[2], along_z[0], along_z[10], pair]
     for peer in peers:
         pl.semaphore_signal(barrier, inc=1, device_id=peer, device_id_type=MESH)
 
@@ -85,6 +91,8 @@
     other_cols = pl.ds(pl.multiple_of(HALF * oc, 128), HALF)
     w_copy = pltpu.make_async_copy(w_ref.at[:, own_cols], w_own, local_sem.at[0])
     w_copy.start()
+
+    g_copy.wait()
 
     tile = x % 2
     first = WIDE * (x // 2) + 128 * tile
@@ -102,13 +110,13 @@
         rolled = pltpu.roll(window.astype(f32), width - (off - start), axis=1)
         pf[d] = jnp.where(keep, rolled[:, :128], 0.0)
 
-    pl.semaphore_wait(barrier, len(peers))
-    send(pf.at[pl.ds(16 * oc, 16)], pf_in, pair_s.at[1], pair_r.at[1], pair)
-
+    h_copy.wait()
     for half in range(2):
         hidden = h_ref[:, HALF * half:HALF * (half + 1)].astype(f32)
         act_f[half] = gelu_value(hidden).astype(bf16).astype(f32)
 
+    pl.semaphore_wait(barrier, len(peers))
+    send(pf.at[pl.ds(16 * oc, 16)], pf_in, pair_s.at[1], pair_r.at[1], pair)
     send(act_f.at[oc], act_in, pair_s.at[0], pair_r.at[0], pair)
 
     def rows_of(ys, zs_):
@@ -392,7 +400,6 @@
     gather(3, 1)
     features_here()
     gather(2, 3)
-    turned()
     gather(2, 4)
     product(0)
     reduce_step(0, 0)
@@ -411,6 +418,7 @@
     reduce_step(1, 2)
     reduce_step(1, 3)
     reduce_step(1, 4)
+    turned()
     gathered()
     weight_grad(0)
     weight_grad(1)
@@ -421,36 +429,36 @@
     sum_send(0)
     reduce_step(2, 1)
     reduce_step(2, 2)
+    reduce_step(2, 3)
+    reduce_step(2, 4)
     sum_wait(0)
     sum_send(1)
-    reduce_step(2, 3)
-    reduce_step(2, 4)
     reduce_step(3, 0)
     reduce_step(3, 1)
+    reduce_step(3, 2)
     sum_wait(1)
     sum_send(2)
-    reduce_step(3, 2)
     reduce_step(3, 3)
     reduce_step(3, 4)
     reduce_z(0)
     reduce_z(1)
     reduce_z(2)
-    sum_wait(2)
-    sum_send(3)
     reduce_z(3)
     reduce_z(4)
     reduce_z2(0)
     reduce_z2(1)
+    sum_wait(2)
+    sum_send(3)
     reduce_z2(2)
     reduce_z2(3)
     reduce_z2(4)
-    sum_wait(3)
     reduce_end(0)
-    outs = scaled()
     reduce_end(1)
     reduce_end(2)
     reduce_end(3)
     reduce_end(4)
+    sum_wait(3)
+    outs = scaled()
 
     for k in range(NK):
         arrived(fin_in.at[k], fin_s.at[k], fin_r.at[k])
@@ -483,7 +491,7 @@
     vmem = pltpu.VMEM
     n_sum = 1 + (NX - 1) + (NY - 1) + (NZL * NZH - 1)
     sems = [
-        (3,), (3,), (3,), (NK,), (NK,), (NY,), (NY,), (2,), (NZH,), (NX, NZH), (NX, NZH),
+        (5,), (3,), (3,), (NK,), (NK,), (NY,), (NY,), (2,), (NZH,), (NX, NZH), (NX, NZH),
         (NX, NZH), (NX, NZH), (2, 4, 5), (2, 4, 5), (5,), (5,), (2, 4, NK), (2, 4, NK),
         (NK, 4), (NK, 4), (NK,), (NK,), (n_sum,), (n_sum,),
     ]
@@ -494,8 +502,8 @@
             jax.ShapeDtypeStruct(w_down.T.shape, bf16),
         ),
         in_specs=[
-            pl.BlockSpec(memory_space=pltpu.VMEM),
-            pl.BlockSpec(memory_space=pltpu.VMEM),
+            pl.BlockSpec(memory_space=pl.ANY),
+            pl.BlockSpec(memory_space=pl.ANY),
             pl.BlockSpec(memory_space=pl.ANY),
         ],
         out_specs=(
@@ -503,6 +511,8 @@
             pl.BlockSpec(memory_space=pl.ANY),
         ),
         scratch_shapes=[
+            vmem((8, 2 * HALF), bf16),
+            vmem((8, D), bf16),
             vmem((2, 8, HALF), f32),
             vmem((2, 8, HALF), f32),
             vmem((8, HALF), f32),
@@ -533,7 +543,7 @@
             vmem((n_sum, 8, 128), f32),
         ] + [dma(s) for s in sems],
         compiler_params=pltpu.CompilerParams(
-            collective_id=0, has_side_effects=True, vmem_limit_bytes=50 * 1024 * 1024
+            collective_id=0, has_side_effects=True, vmem_limit_bytes=63 * 1024 * 1024
         ),
         cost_estimate=pl.CostEstimate(
             flops=4 * TOKENS * 2 * HALF * WIDE, bytes_accessed=6 << 20, transcendentals=0

time: 78.5 us -> 77.4 us (0.986)
  local copies, waits for them, and re-layouts: 4.62 us -> 3.76 us
    unnamed x8 -> x2, local copies, waits for them, and re-layouts: 4.62 us -> 3.76 us
where the time goes in v3:
time: 77.4 us; the launch traced here: 77.2 us
  Pallas kernels  72.8 us (94%)
  local copies, waits for them, and re-layouts  3.76 us (5%)
    pallas_call x1, Pallas kernels, local(): pl.pallas_call(kernel, out_shape=(jax.ShapeDtypeStruct(hidden_pre.shape,...  72.8 us
    unnamed x2, local copies, waits for them, and re-layouts  3.76 us

profile of v3, /device:TPU:1, one launch (start us, length us, event | category | flops | bytes accessed | tf_op | source)
XLA Modules:
  0.0 77.2 jit_solution(12807067737413368673)
XLA Ops:
  0.6 72.8 %shard_map.50 = (bf16[8,2560]{1,0:T(8,128)(2,1)}, bf16[232,2560]{1,0:T(8,128)(2,1)}) custom-call(bf16[8,2560]{1,0:T(8,128)(2,1)} %h_hbm.1, bf16[8,14848]{1,0:T(8,128)(2,1)} %g_hbm.1, bf16[232,2560]{1,0:T(8,128)(2,1)} %bitcast.3), custom_call_target="tpu_custom_call" | custom-call | flops 1216348160 | bytes 6291456 | tf_op jit(solution)/shard_map/pallas_call | solution.py:498
  73.4 1.4 %copy.7 = bf16[8,2560]{1,0:T(8,128)(2,1)} copy(bf16[8,2560]{1,0:T(8,128)(2,1)} %get-tuple-element.8) | data formatting | bytes 81920
  74.8 2.4 %copy.8 = bf16[2560,232]{0,1:T(8,128)(2,1)} copy(bf16[2560,232]{0,1:T(8,128)(2,1)} %bitcast.2) | data formatting | bytes 2375680

commit v4 on v3

--- a/solution.py
+++ b/solution.py
@@ -80,10 +80,12 @@
     along_z = [at(zl_=p % NZL, zh_=p // NZL) for p in along_z]
     along_y = [at(y_=(y + r) % NY) for r in range(1, NY)]
     along_x = [at(x_=(x + r) % NX) for r in range(1, NX)]
+    across_x = [at(x_=(x + r) % NX, c_=oc) for r in range(1, NX)]
     peers = [along_z[r - 1] for r in (6, 5, 7, 4, 8, 3, 9)]
     peers += [along_y[r - 1] for r in (4, 3, 5, 2, 6)]
     peers += [along_z[r - 1] for r in (2, 10)] + [along_x[1]]
     peers += [along_y[0], along_y[6], along_x[0], along_x[2], along_z[0], along_z[10], pair]
+    peers += across_x
     for peer in peers:
         pl.semaphore_signal(barrier, inc=1, device_id=peer, device_id_type=MESH)
 
@@ -330,8 +332,7 @@
         ar_src[0] = part if k == 0 else ar_src[0] + part
 
     stages = (
-        [pair],
-        [at(x_=(x + r) % NX) for r in range(1, NX)],
+        [pair] + along_x + across_x,
         [at(y_=(y + r) % NY) for r in range(1, NY)],
         along_z,
     )
@@ -350,7 +351,7 @@
         ar_src[i + 1] = val
 
     def scaled():
-        sumsq = jnp.sum(ar_src[4])
+        sumsq = jnp.sum(ar_src[3])
         rms = jnp.sqrt(jnp.full((8, 128), sumsq, f32) / (float(FF) * float(D)) + 1e-06)
         scale = jnp.minimum(1.0, 1.0 / rms)[0:1, 0:1]
         gdv[:, own_cols] = (raw[c] * scale).astype(bf16)
@@ -431,13 +432,11 @@
     reduce_step(2, 2)
     reduce_step(2, 3)
     reduce_step(2, 4)
-    sum_wait(0)
-    sum_send(1)
     reduce_step(3, 0)
     reduce_step(3, 1)
     reduce_step(3, 2)
-    sum_wait(1)
-    sum_send(2)
+    sum_wait(0)
+    sum_send(1)
     reduce_step(3, 3)
     reduce_step(3, 4)
     reduce_z(0)
@@ -447,8 +446,8 @@
     reduce_z(4)
     reduce_z2(0)
     reduce_z2(1)
-    sum_wait(2)
-    sum_send(3)
+    sum_wait(1)
+    sum_send(2)
     reduce_z2(2)
     reduce_z2(3)
     reduce_z2(4)
@@ -457,7 +456,7 @@
     reduce_end(2)
     reduce_end(3)
     reduce_end(4)
-    sum_wait(3)
+    sum_wait(2)
     outs = scaled()
 
     for k in range(NK):
@@ -489,7 +488,7 @@
 def local(hidden_pre, grad_out, w_down):
     dma = pltpu.SemaphoreType.DMA
     vmem = pltpu.VMEM
-    n_sum = 1 + (NX - 1) + (NY - 1) + (NZL * NZH - 1)
+    n_sum = 2 * NX - 1 + (NY - 1) + (NZL * NZH - 1)
     sems = [
         (5,), (3,), (3,), (NK,), (NK,), (NY,), (NY,), (2,), (NZH,), (NX, NZH), (NX, NZH),
         (NX, NZH), (NX, NZH), (2, 4, 5), (2, 4, 5), (5,), (5,), (2, 4, NK), (2, 4, NK),
@@ -543,7 +542,7 @@
             vmem((n_sum, 8, 128), f32),
         ] + [dma(s) for s in sems],
         compiler_params=pltpu.CompilerParams(
-            collective_id=0, has_side_effects=True, vmem_limit_bytes=63 * 1024 * 1024
+            collective_id=0, has_side_effects=True, vmem_limit_bytes=53632 * 1024
         ),
         cost_estimate=pl.CostEstimate(
             flops=4 * TOKENS * 2 * HALF * WIDE, bytes_accessed=6 << 20, transcendentals=0

time: 77.4 us -> 76.3 us (0.986)
    unnamed x2 -> x6, local copies, waits for them, and re-layouts: 3.76 us -> 3.35 us
where the time goes in v4:
time: 76.3 us; the launch traced here: 76.1 us
  Pallas kernels  72.1 us (94%)
  local copies, waits for them, and re-layouts  3.35 us (4%)
    pallas_call x1, Pallas kernels, local(): pl.pallas_call(kernel, out_shape=(jax.ShapeDtypeStruct(hidden_pre.shape,...  72.1 us
    unnamed x6, local copies, waits for them, and re-layouts  3.35 us

profile of v4, /device:TPU:1, one launch (start us, length us, event | category | flops | bytes accessed | tf_op | source)
XLA Modules:
  0.0 76.1 jit_solution(530043532514576336)
XLA Ops:
  0.6 0.0 copy-start
  0.6 0.9 %copy-done = bf16[8,14848]{1,0:T(8,128)(2,1)S(1)} copy-done((bf16[8,14848]{1,0:T(8,128)(2,1)S(1)}, bf16[8,14848]{1,0:T(8,128)(2,1)}, u32[]{:S(2)}) %copy-start) | copy-done | bytes 237592
  1.6 0.0 copy-start.1
  1.6 0.8 %copy-done.1 = bf16[8,2560]{1,0:T(8,128)(2,1)S(1)} copy-done((bf16[8,2560]{1,0:T(8,128)(2,1)S(1)}, bf16[8,2560]{1,0:T(8,128)(2,1)}, u32[]{:S(2)}) %copy-start.1) | copy-done | bytes 40984
  2.4 72.1 %shard_map.50 = (bf16[8,2560]{1,0:T(8,128)(2,1)S(1)}, bf16[232,2560]{1,0:T(8,128)(2,1)S(1)}) custom-call(bf16[8,2560]{1,0:T(8,128)(2,1)S(1)} %copy-done.1, bf16[8,14848]{1,0:T(8,128)(2,1)S(1)} %copy-done, bf16[232,2560]{1,0:T(8,128)(2,1)} %bitcast.3), custom_call_target="tpu_custom_call" | custom-call | flops 1216348160 | bytes 6291456 | tf_op jit(solution)/shard_map/pallas_call | solution.py:497
  74.5 0.6 copy.7
  75.1 1.0 %copy.8 = bf16[2560,232]{0,1:T(8,128)(2,1)} copy(bf16[2560,232]{0,1:T(8,128)(2,1)S(1)} %bitcast.2) | data formatting | bytes 2375680
Async XLA Ops:
  0.6 0.9 %copy-start = (bf16[8,14848]{1,0:T(8,128)(2,1)S(1)}, bf16[8,14848]{1,0:T(8,128)(2,1)}, u32[]{:S(2)}) copy-start(bf16[8,14848]{1,0:T(8,128)(2,1)} %g_hbm.1) | copy-start | bytes 712708
  1.6 0.8 %copy-start.1 = (bf16[8,2560]{1,0:T(8,128)(2,1)S(1)}, bf16[8,2560]{1,0:T(8,128)(2,1)}, u32[]{:S(2)}) copy-start(bf16[8,2560]{1,0:T(8,128)(2,1)} %h_hbm.1) | copy-start | bytes 122884

commit v5 on v4

--- a/solution.py
+++ b/solution.py
@@ -371,8 +371,6 @@
             slope[half] = gelu_slope(h_ref[:, HALF * half:HALF * (half + 1)].astype(f32))
 
     send(w_ref.at[:, other_cols], w_in, pair_s.at[2], pair_r.at[2], pair)
-    slopes()
-    weights()
     gather(1, 0)
     features_z()
     features_x(0)
@@ -383,6 +381,8 @@
     gather(2, 0)
     gather(1, 2)
     features_pair(0)
+    slopes()
+    weights()
     features_x(1)
     features_x(3)
     gather(1, 1)

time: 76.3 us -> 75.7 us (level)
  no operation moved by 1% of the time
where the time goes in v5:
time: 75.7 us; the launch traced here: 75.5 us
  Pallas kernels  71.5 us (94%)
  local copies, waits for them, and re-layouts  3.35 us (4%)
    pallas_call x1, Pallas kernels, local(): pl.pallas_call(kernel, out_shape=(jax.ShapeDtypeStruct(hidden_pre.shape,...  71.5 us
    unnamed x6, local copies, waits for them, and re-layouts  3.35 us

profile of v5, /device:TPU:1, one launch (start us, length us, event | category | flops | bytes accessed | tf_op | source)
XLA Modules:
  0.0 75.5 jit_solution(4672144954598124264)
XLA Ops:
  0.6 0.0 copy-start
  0.6 0.9 %copy-done = bf16[8,14848]{1,0:T(8,128)(2,1)S(1)} copy-done((bf16[8,14848]{1,0:T(8,128)(2,1)S(1)}, bf16[8,14848]{1,0:T(8,128)(2,1)}, u32[]{:S(2)}) %copy-start) | copy-done | bytes 237592
  1.6 0.0 copy-start.1
  1.6 0.8 %copy-done.1 = bf16[8,2560]{1,0:T(8,128)(2,1)S(1)} copy-done((bf16[8,2560]{1,0:T(8,128)(2,1)S(1)}, bf16[8,2560]{1,0:T(8,128)(2,1)}, u32[]{:S(2)}) %copy-start.1) | copy-done | bytes 40984
  2.4 71.5 %shard_map.50 = (bf16[8,2560]{1,0:T(8,128)(2,1)S(1)}, bf16[232,2560]{1,0:T(8,128)(2,1)S(1)}) custom-call(bf16[8,2560]{1,0:T(8,128)(2,1)S(1)} %copy-done.1, bf16[8,14848]{1,0:T(8,128)(2,1)S(1)} %copy-done, bf16[232,2560]{1,0:T(8,128)(2,1)} %bitcast.3), custom_call_target="tpu_custom_call" | custom-call | flops 1216348160 | bytes 6291456 | tf_op jit(solution)/shard_map/pallas_call | solution.py:497
  73.8 0.6 copy.7
  74.4 1.0 %copy.8 = bf16[2560,232]{0,1:T(8,128)(2,1)} copy(bf16[2560,232]{0,1:T(8,128)(2,1)S(1)} %bitcast.2) | data formatting | bytes 2375680
Async XLA Ops:
  0.6 0.9 %copy-start = (bf16[8,14848]{1,0:T(8,128)(2,1)S(1)}, bf16[8,14848]{1,0:T(8,128)(2,1)}, u32[]{:S(2)}) copy-start(bf16[8,14848]{1,0:T(8,128)(2,1)} %g_hbm.1) | copy-start | bytes 712708
  1.6 0.8 %copy-start.1 = (bf16[8,2560]{1,0:T(8,128)(2,1)S(1)}, bf16[8,2560]{1,0:T(8,128)(2,1)}, u32[]{:S(2)}) copy-start(bf16[8,2560]{1,0:T(8,128)(2,1)} %h_hbm.1) | copy-start | bytes 122884
